TPU v7x, 512 devices: a whole 4x4x16 slice. The times are simulated.
512 devices in a mesh: band: 16 (over z_lo, core), tile: 32 (over x, z_hi, y).
Axes of the slice: x: 4, y: 4, z: 16 (z_hi: 2, z_lo: 8; z = z_hi * 8 + z_lo), core: 2. Of those that a mesh axis runs over, the one named last changes fastest.
Arguments:
- raw_traces: bfloat16 [32, 4096, 2048], P('tile', 'band'), may hold values from -6 to 6
- bin_owner: int32 [32, 4096, 1], P('tile'), may hold values from 0 to 31; in each aligned block of 4096 rows (0 to 4095, 4096 to 8191, ..., all dimensions but the last counted through in order) at most 256 rows name the same one
- bin_offset: int32 [32, 4096], P('tile'), may hold values from 0 to 8191
Outputs:
- multiples: float32 [160, 2, 512, 512], P('band', None, 'tile')
Inputs may be any that keep to these rules, and one draw needn't show every extreme that they name: `bin_owner`: in each tile's list of 4096 traces at most 256 are binned into one tile, and some tile receives exactly 256.
All inputs are finite; a program needn't handle non-finite values.
Results may differ from a plain program's by a relative error of at most 0.0067.
Values may be sent and summed in bfloat16 or wider, within the bound.
A program may use at most 128 MiB of HBM per device.

v0:
```python
import math

import jax
import jax.numpy as jnp
from jax import lax
from jax.sharding import PartitionSpec as P

NG = 512
NT = 2048
FB = 10


def twiddle_grid(band_count):
    time_index = jnp.arange(NT, dtype=jnp.int32)
    freq_index = jnp.arange(band_count * FB, dtype=jnp.int32).reshape(band_count, FB) + 1
    phase_angle = (time_index[:, None, None] * freq_index[None, :, :] % NT).astype(jnp.float32) * (
        2.0 * math.pi / NT
    )
    norm_factor = 1.0 / math.sqrt(NT)
    stacked = jnp.stack(
        [jnp.cos(phase_angle) * norm_factor, -jnp.sin(phase_angle) * norm_factor], axis=2
    )
    return stacked.reshape(NT, band_count * 2 * FB).astype(jnp.bfloat16)


def complex_rows(left_rows, right_rows):
    real_real = jnp.einsum(
        "fik,fjk->fij", left_rows[:, 0], right_rows[:, 0], preferred_element_type=jnp.float32
    )
    imag_imag = jnp.einsum(
        "fik,fjk->fij", left_rows[:, 1], right_rows[:, 1], preferred_element_type=jnp.float32
    )
    real_imag = jnp.einsum(
        "fik,fjk->fij", left_rows[:, 0], right_rows[:, 1], preferred_element_type=jnp.float32
    )
    imag_real = jnp.einsum(
        "fik,fjk->fij", left_rows[:, 1], right_rows[:, 0], preferred_element_type=jnp.float32
    )
    return jnp.stack([real_real - imag_imag, real_imag + imag_real], axis=1)


def per_device(raw_traces, bin_owner, bin_offset):
    band_count = lax.axis_size("band")
    tile_count = lax.axis_size("tile")
    traces = raw_traces[0]
    trace_count = traces.shape[0]
    out_scale = 1.0 / math.sqrt(NG)
    twiddle = twiddle_grid(band_count)
    spectra = jnp.dot(traces, twiddle, preferred_element_type=jnp.float32).astype(jnp.bfloat16)
    spectra = spectra.reshape(trace_count, band_count, 2 * FB)
    received = lax.all_to_all(spectra, "band", split_axis=1, concat_axis=0, tiled=True).reshape(
        -1, 2 * FB
    )
    owners = bin_owner[0, :, 0]
    offset = bin_offset[0]
    list_length = owners.shape[0]
    capacity = 2 * list_length // tile_count
    cells_dev = NG * NG // tile_count
    owner_hits = (owners[:, None] == jnp.arange(tile_count, dtype=jnp.int32)[None, :]).astype(
        jnp.int32
    )
    slot_rank = jnp.sum((jnp.cumsum(owner_hits, axis=0) - 1) * owner_hits, axis=1)
    slot_index = owners * capacity + slot_rank
    outgoing = (
        jnp.zeros((2 * FB, tile_count * capacity), jnp.bfloat16).at[:, slot_index].set(received.T)
    )
    outgoing = outgoing.reshape(2 * FB, tile_count, capacity)
    labels = jnp.full((tile_count * capacity,), cells_dev, jnp.int32).at[slot_index].set(offset)
    labels = labels.reshape(tile_count, capacity)
    arrived = lax.all_to_all(outgoing, "tile", split_axis=1, concat_axis=1, tiled=True)
    arrived_cells = lax.all_to_all(labels, "tile", split_axis=0, concat_axis=0, tiled=True).reshape(
        -1
    )
    slot_values = arrived.reshape(2 * FB, -1).T.astype(jnp.float32)
    cell_sums = jax.ops.segment_sum(slot_values, arrived_cells, cells_dev + 1)[:cells_dev]
    counts = jax.ops.segment_sum(
        jnp.ones(arrived_cells.shape, jnp.float32), arrived_cells, cells_dev + 1
    )[:cells_dev]
    grid_field = (cell_sums / jnp.maximum(counts, 1.0)[:, None]).astype(jnp.bfloat16)
    row_block = NG // tile_count
    grid_field = grid_field.T.reshape(2, FB, row_block, NG).transpose(1, 0, 2, 3)
    gathered = lax.all_gather(grid_field, "tile", axis=2, tiled=True)
    symmetric_all = (
        0.5 * (gathered.astype(jnp.float32) + jnp.swapaxes(gathered, 2, 3).astype(jnp.float32))
    ).astype(jnp.bfloat16)
    first_row = lax.axis_index("tile") * row_block
    symmetric = lax.dynamic_slice_in_dim(symmetric_all, first_row, row_block, 2)
    result = complex_rows(symmetric, symmetric_all) * out_scale
    return result


def solution(mesh):
    return jax.shard_map(
        per_device,
        mesh=mesh,
        in_specs=(P("tile", "band", None), P("tile", None, None), P("tile", None)),
        out_specs=P("band", None, "tile", None),
        check_vma=False,
    )
```

profile of v0, /device:TPU:1, one launch (start us, length us, event | category | flops | bytes accessed | tf_op | source)
XLA Modules:
  0.0 585.3 jit_solution(13382952497239670292)
XLA Ops:
  6.5 5.7 multiply_convert_fusion.1
  12.3 0.8 copy.35
  13.2 1.3 convert_element_type.63
  14.5 1.9 fusion.20
  16.4 0.7 reshape.161
  17.1 14.0 %all-to-all-start.1 = ((bf16[256,16,20]{0,2,1:T(8,128)(2,1)}), bf16[256,16,20]{0,2,1:T(8,128)(2,1)S(1)}, u32[]{:S(2)}, u32[]{:S(2)}) async-start(bf16[256,16,20]{0,2,1:T(8,128)(2,1)} %reshape.161), calls=%async_computation.1 | async-start | bytes 393216 | tf_op jit(solution)/shard_map/all_to_all | solution.py:51
  31.2 9.2 %reduce-window.6 = s32[32,32,128]{2,1,0:T(8,128)S(1)} reduce-window(s32[32,32,128]{2,1,0:T(8,128)S(1)} %fusion.26, s32[]{:T(128)} %constant.21.clone.1), window={size=1x1x128 pad=0_0x0_0x127_0}, to_apply=%region_0.1 | reduce-window | flops 16646144 | bytes 1048580 | tf_op jit(solution)/shard_map/reduce-window
  40.4 0.8 slice_reduce_fusion
  41.6 0.3 fusion.25
  42.0 16.3 %scatter_custom_fusion = s32[8192]{0:T(1024)} fusion(s32[4096]{0:T(1024)S(1)} %bitcast.102, s32[4096]{0:T(1024)} %bitcast.104, s32[]{:T(128)} %constant.19.clone.1), kind=kCustom, calls=%fused_computation.56 | custom fusion | bytes 33280 | tf_op jit(solution)/shard_map/scatter | solution.py:68
  58.2 12.8 %all-to-all-start = ((s32[32,1,256]{2,1,0:T(1,128)}), s32[32,1,256]{2,1,0:T(1,128)S(1)}, u32[]{:S(2)}, u32[]{:S(2)}) async-start(s32[32,1,256]{2,1,0:T(1,128)} %bitcast.7), calls=%async_computation | async-start | bytes 65536 | tf_op jit(solution)/shard_map/all_to_all | solution.py:71
  71.1 0.5 copy.46
  71.6 11.6 %scatter_custom_fusion.1 = bf16[20,8192]{0,1:T(8,128)(2,1)S(1)} fusion(s32[4096]{0:T(1024)S(1)} %bitcast.103, bf16[4096,20]{1,0:T(8,128)(2,1)S(1)} %bitcast.94, bf16[]{:T(256)} %constant.14.clone.1), kind=kCustom, calls=%fused_computation.37 | custom fusion | bytes 327682 | tf_op jit(solution)/shard_map/scatter | solution.py:65
  83.1 1.6 copy.38
  84.7 2.2 all-to-all-done
  87.0 14.2 %all-to-all-start.2 = ((bf16[20,32,256]{2,0,1:T(8,128)(2,1)}), bf16[20,32,256]{2,0,1:T(8,128)(2,1)S(1)}, u32[]{:S(2)}, u32[]{:S(2)}) async-start(bf16[20,32,256]{2,0,1:T(8,128)(2,1)} %copy.38), calls=%async_computation.2 | async-start | bytes 786432 | tf_op jit(solution)/shard_map/all_to_all | solution.py:70
  101.3 53.6 %scatter_custom_fusion.3 = f32[8193]{0:T(1024)S(1)} fusion(s32[8192]{0:T(1024)S(1)} %bitcast.100, f32[8192]{0:T(1024)S(1)} %broadcast.171, f32[]{:T(128)} %constant.18.clone.1), kind=kCustom, calls=%fused_computation.53 | custom fusion | flops 8192 | bytes 32776 | tf_op jit(solution)/shard_map/scatter-add | solution.py:76
  155.0 0.5 copy.49
  155.5 2.7 copy.40
  158.2 55.6 %scatter_custom_fusion.2 = f32[8193,20]{1,0:T(8,128)} fusion(s32[8192]{0:T(1024)S(1)} %bitcast.101, f32[8192,20]{1,0:T(8,128)} %copy.40, f32[]{:T(128)} %constant.18.clone.1), kind=kCustom, calls=%fused_computation.15 | custom fusion | flops 163840 | bytes 655952 | tf_op jit(solution)/shard_map/scatter-add | solution.py:75
  213.8 5.0 fusion.9
  218.8 0.9 copy.41
  219.9 1.1 copy.42
  221.0 297.0 %all-gather.2.cloned.1.call-done = bf16[10,2,512,512]{3,1,0,2:T(2,128)(2,1)} async-done(((bf16[10,2,16,512]{3,1,0,2:T(2,128)(2,1)}), bf16[10,2,512,512]{3,1,0,2:T(2,128)(2,1)}) %all-gather.2.cloned.1.call-update) | async-done | bytes 10485776 | tf_op jit(solution)/shard_map/all_gather | solution.py:82
  518.0 26.0 %copy.43 = bf16[10,2,512,512]{2,3,0,1:T(8,128)(2,1)} copy(bf16[10,2,512,512]{3,1,0,2:T(2,128)(2,1)} %all-gather.2.cloned.1.call-done) | data formatting | bytes 20971520 | tf_op jit(solution)/shard_map/all_gather | solution.py:82
  544.0 16.3 %copy.44 = f32[10,2,512,512]{3,2,0,1:T(8,128)} copy(bf16[10,2,512,512]{2,3,0,1:T(8,128)(2,1)} %copy.43) | data formatting | bytes 31457280 | tf_op jit(solution)/shard_map/convert_element_type | solution.py:84
  560.3 11.2 %fusion.1 = bf16[10,2,512,512]{3,2,0,1:T(8,128)(2,1)S(1)} fusion(f32[10,2,512,512]{3,2,0,1:T(8,128)} %copy.44, bf16[10,2,512,512]{2,3,0,1:T(8,128)(2,1)} %copy.43), kind=kLoop, calls=%fused_computation.6 | loop fusion | flops 20971520 | bytes 41943040 | tf_op jit(solution)/shard_map/convert_element_type | solution.py:85
  571.6 1.5 fusion.3
  573.0 1.5 fusion.2
  574.5 1.5 fusion.17
  576.0 1.5 fusion.19
  577.6 0.9 copy.45
  (23 shorter events, 1.1 us)
Async XLA Ops:
  6.5 8.0 %copy-start = (bf16[1,256,2048]{2,1,0:T(8,128)(2,1)S(1)}, bf16[1,256,2048]{2,1,0:T(8,128)(2,1)}, u32[]{:S(2)}) copy-start(bf16[1,256,2048]{2,1,0:T(8,128)(2,1)} %param.3) | copy-start | bytes 3145732
  13.1 18.0 %copy-start.2 = (s32[1,4096,1]{1,2,0:T(1,128)S(1)}, s32[1,4096,1]{1,2,0:T(1,128)}, u32[]{:S(2)}) copy-start(s32[1,4096,1]{1,2,0:T(1,128)} %param.4) | copy-start | bytes 49156
  17.1 41.2 %all-to-all-start.1 = ((bf16[256,16,20]{0,2,1:T(8,128)(2,1)}), bf16[256,16,20]{0,2,1:T(8,128)(2,1)S(1)}, u32[]{:S(2)}, u32[]{:S(2)}) async-start(bf16[256,16,20]{0,2,1:T(8,128)(2,1)} %reshape.161), calls=%async_computation.1 | async-start | bytes 393216 | tf_op jit(solution)/shard_map/all_to_all | solution.py:51
  58.2 28.8 %all-to-all-start = ((s32[32,1,256]{2,1,0:T(1,128)}), s32[32,1,256]{2,1,0:T(1,128)S(1)}, u32[]{:S(2)}, u32[]{:S(2)}) async-start(s32[32,1,256]{2,1,0:T(1,128)} %bitcast.7), calls=%async_computation | async-start | bytes 65536 | tf_op jit(solution)/shard_map/all_to_all | solution.py:71
  87.0 67.9 %all-to-all-start.2 = ((bf16[20,32,256]{2,0,1:T(8,128)(2,1)}), bf16[20,32,256]{2,0,1:T(8,128)(2,1)S(1)}, u32[]{:S(2)}, u32[]{:S(2)}) async-start(bf16[20,32,256]{2,0,1:T(8,128)(2,1)} %copy.38), calls=%async_computation.2 | async-start | bytes 786432 | tf_op jit(solution)/shard_map/all_to_all | solution.py:70
  101.2 416.8 %all-gather.2.cloned.1.call-start = ((), (), s32[]{:S(2)}) async-start(), calls=%async_computation.3 | async-start | bytes 10813440 | tf_op jit(solution)/shard_map/all_gather | solution.py:82
  574.5 3.9 copy-start.1
Sparse Core Ops, SparseCore 0:
  221.1 296.8 all-gather.1
where the time goes:
time: 587 us; the launch traced here: 585 us
  waiting for transfers between devices  299 us (51%)
  other arithmetic  141 us (24%)
  local copies, waits for them, and re-layouts  82.1 us (14%)
  starting transfers between devices  41.1 us (7%)
  between operations  13.6 us (2%)
  matrix products  7.75 us (1%)
    all_gather x1, waiting for transfers between devices, per_device(): gathered = lax.all_gather(grid_field, 'tile', axis=2, tiled=True)  297 us
    scatter-add x1, other arithmetic, per_device(): jax.ops.segment_sum(slot_values, arrived_cells, cells_dev + 1)[:cells_dev]  55.6 us
    scatter-add x1, other arithmetic, per_device(): jax.ops.segment_sum(jnp.ones(arrived_cells.shape, jnp.float32), arrived_c...  53.6 us
    all_gather x1, local copies, waits for them, and re-layouts, per_device(): gathered = lax.all_gather(grid_field, 'tile', axis=2, tiled=True)  26 us
    convert_element_type x1, local copies, waits for them, and re-layouts, per_device(): gathered.astype(jnp.float32)  16.3 us
    scatter x1, local copies, waits for them, and re-layouts, per_device(): jnp.full((tile_count * capacity,), cells_dev, jnp.int32).at[slot_index]  16.3 us
    another operation x3, other arithmetic  15.1 us
    all_to_all x1, starting transfers between devices, per_device(): lax.all_to_all(outgoing, 'tile', split_axis=1, concat_axis=1, tiled=True)  14.2 us
  transfers between devices with their start and end apart: 4, of which 2 were waited for; matrix products, arithmetic and copies ran while one was open for 16% of the time, Pallas kernels for 0%

commit v1 on v0

v1 whole, which is shorter than its diff:
```python
import math

import jax
import jax.numpy as jnp
import numpy as np
from jax import lax
from jax.experimental import pallas as pl
from jax.experimental.pallas import tpu as pltpu
from jax.sharding import PartitionSpec as P

NG = 512
NT = 2048
FB = 10
NB = 16
NTILE = 32
HF = 5
ROWS = 16
CH = 256
MESH = pl.DeviceIdType.MESH
F32 = jnp.float32
BF16 = jnp.bfloat16


def twiddle_rows():
    time = np.arange(NT, dtype=np.int64)
    table = np.zeros((2, NB, ROWS, NT), np.float64)
    for half in range(2):
        for band in range(NB):
            for i in range(HF):
                k = band * FB + half * HF + i + 1
                angle = 2.0 * math.pi * ((time * k) % NT) / NT
                table[half, band, 2 * i] = np.cos(angle) / math.sqrt(NT)
                table[half, band, 2 * i + 1] = -np.sin(angle) / math.sqrt(NT)
    return table.reshape(2 * NB * ROWS, NT).astype(np.float32).astype(jnp.bfloat16)


def tile_of(chip, half):
    return (chip // 4) * 8 + half * 4 + chip % 4


def shift_of(z):
    return (z * 5) % 16


def handler_chip(n, z):
    n0 = (n + 16 - shift_of(z)) % 16
    x = n0 % 4
    y = (n0 // 4 + x) % 4
    return x * 4 + y


def handler_number(chip, z):
    x = chip // 4
    y = chip % 4
    return (4 * ((y + 4 - x) % 4) + x + shift_of(z)) % 16


def onehot_groups(chunks, key_row, lo_row, l_ref, r_ref):
    low = lax.broadcasted_iota(jnp.int32, (CH, CH), 0).astype(F32).astype(BF16)
    zero = jnp.zeros((ROWS, CH), BF16)
    for n, chunk in enumerate(chunks):
        wide = chunk.astype(F32)
        key = jnp.broadcast_to(wide[key_row : key_row + 1], (ROWS, CH)).astype(BF16)
        lo = jnp.broadcast_to(wide[lo_row : lo_row + 1], (ROWS, CH)).astype(BF16)
        cols = slice(n * CH, (n + 1) * CH)
        for k in range(32):
            l_ref[k * ROWS : (k + 1) * ROWS, cols] = jnp.where(key == BF16(k), chunk, zero)
        lo_all = jnp.concatenate([lo] * (CH // ROWS), axis=0)
        r_ref[:, cols] = jnp.where(low == lo_all, BF16(1), BF16(0))


def nt_dot(left, right):
    return lax.dot_general(left, right, (((1,), (1,)), ((), ())), preferred_element_type=F32)


def kernel(
    raw_ref, tw_ref, own_ref, off_ref, out_ref,
    send1, rc1, l_ref, r_ref, acc_ref, send2, rc2, g_ref, rc3, s1, s2, mout,
    sem1s, sem1r, sem2s, sem2r, sem3s, sem3r, sem4s, sem4r,
):
    band = lax.axis_index("band")
    tile = lax.axis_index("tile")
    x = tile // 8
    half = (tile // 4) % 2
    y = tile % 4
    chip = x * 4 + y
    zlo = band // 2
    core = band % 2
    z = half * 8 + zlo
    me1 = half * NB + band

    def at_column(d):
        return {"band": d % NB, "tile": x * 8 + (d // NB) * 4 + y}

    def at_plane(c, h):
        return {"band": band, "tile": tile_of(c, h)}

    barrier = pltpu.get_barrier_semaphore()

    def greet_column(r, carry):
        d = (me1 + r) % 32
        pl.semaphore_signal(barrier, inc=1, device_id=at_column(d), device_id_type=MESH)
        return carry

    def greet_plane(r, carry):
        c = (chip + r) % 16
        pl.semaphore_signal(barrier, inc=1, device_id=at_plane(c, half), device_id_type=MESH)
        pl.semaphore_signal(barrier, inc=1, device_id=at_plane(c, 1 - half), device_id_type=MESH)
        return carry

    lax.fori_loop(1, 32, greet_column, 0)
    lax.fori_loop(1, 16, greet_plane, 0)

    ids = lax.broadcasted_iota(jnp.int32, (32, 128), 0)

    def owner_code(t):
        return (t // 8) * 8 + (t % 4) * 2 + (t // 4) % 2

    def count(i, carry):
        row = jnp.broadcast_to(owner_code(own_ref[pl.ds(i, 1), :]), (32, 128))
        before = jnp.where(i < 2 * band, 1.0, 0.0)
        return carry + jnp.where(row == ids, 1.0, 0.0) * before

    counts = lax.fori_loop(0, 32, count, jnp.zeros((32, 128), F32))
    counts = jnp.sum(counts, axis=1, keepdims=True)
    own = jnp.concatenate([own_ref[pl.ds(2 * band, 1), :], own_ref[pl.ds(2 * band + 1, 1), :]], axis=1)
    off = jnp.concatenate([off_ref[pl.ds(2 * band, 1), :], off_ref[pl.ds(2 * band + 1, 1), :]], axis=1)
    own = owner_code(own)
    hits = jnp.broadcast_to(own, (32, CH)) == lax.broadcasted_iota(jnp.int32, (32, CH), 0)
    hits = jnp.where(hits, 1.0, 0.0)
    earlier = lax.broadcasted_iota(jnp.int32, (CH, CH), 0) < lax.broadcasted_iota(jnp.int32, (CH, CH), 1)
    earlier = jnp.where(earlier, 1.0, 0.0).astype(BF16)
    ahead = jnp.dot(hits.astype(BF16), earlier, preferred_element_type=F32)
    rank = jnp.sum(hits * (ahead + counts), axis=0, keepdims=True)
    column = off % NG
    key2 = (column // CH) * 16 + off // NG
    row_id = lax.broadcasted_iota(jnp.int32, (ROWS, CH), 0)
    labels = jnp.where(row_id == 10, 1.0, 0.0)
    for at, value in ((11, own.astype(F32)), (12, rank), (13, key2.astype(F32)), (14, (column % CH).astype(F32))):
        labels = labels + jnp.where(row_id == at, jnp.broadcast_to(value, (ROWS, CH)), 0.0)

    spectra = nt_dot(tw_ref[...], raw_ref[...]).reshape(2 * NB, ROWS, CH)
    send1[...] = (spectra + labels[None]).astype(BF16)

    pl.semaphore_wait(barrier, 31 + 30)

    def copy1(d):
        return pltpu.make_async_remote_copy(
            src_ref=send1.at[d], dst_ref=rc1.at[me1], send_sem=sem1s.at[d], recv_sem=sem1r.at[me1],
            device_id=at_column(d), device_id_type=MESH,
        )

    def start1(r, carry):
        copy1((me1 + r) % 32).start()
        return carry

    own1 = pltpu.make_async_copy(send1.at[me1], rc1.at[me1], sem1r.at[me1])
    own1.start()
    lax.fori_loop(1, 32, start1, 0)

    for lst in range(2):
        def slot(g, carry):
            for n in range(4):
                src = lst * NB + g * 4 + n
                pltpu.make_async_copy(rc1.at[src], rc1.at[src], sem1r.at[src]).wait()
            onehot_groups([rc1[lst * NB + g * 4 + n] for n in range(4)], 11, 12, l_ref, r_ref)
            part = nt_dot(l_ref[...], r_ref[...])
            acc_ref[0] += part
            return carry

        acc_ref[0] = jnp.zeros((512, CH), F32)
        lax.fori_loop(0, 4, slot, 0)
        send2[:, :, lst] = acc_ref[0].reshape(16, 2, ROWS, CH).astype(BF16)

    def copy2(c):
        return pltpu.make_async_remote_copy(
            src_ref=send2.at[c], dst_ref=rc2.at[chip], send_sem=sem2s.at[c], recv_sem=sem2r.at[chip],
            device_id=at_plane(c, half), device_id_type=MESH,
        )

    def start2(r, carry):
        copy2((chip + r) % 16).start()
        return carry

    own2 = pltpu.make_async_copy(send2.at[chip], rc2.at[chip], sem2r.at[chip])
    own2.start()
    lax.fori_loop(1, 16, start2, 0)

    def bin_group(g, carry):
        for n in range(2):
            src = g * 2 + n
            pltpu.make_async_copy(rc2.at[src], rc2.at[src], sem2r.at[src]).wait()
        for h in range(2):
            chunks = [rc2[g * 2 + n // 2, h, n % 2] for n in range(4)]
            onehot_groups(chunks, 13, 14, l_ref, r_ref)
            part = nt_dot(l_ref[...], r_ref[...])
            acc_ref[h] += part
        return carry

    acc_ref[...] = jnp.zeros_like(acc_ref)
    lax.fori_loop(0, 8, bin_group, 0)
    for h in range(2):
        for hi in range(2):
            block = acc_ref[h, hi * 256 : (hi + 1) * 256].reshape(16, ROWS, CH)
            block = block / jnp.maximum(block[:, 10:11, :], 1.0)
            block = jnp.swapaxes(block, 0, 1).astype(BF16)
            for v in range(2 * HF):
                g_ref[v // 2, v % 2, h, :, hi * CH : (hi + 1) * CH] = block[v]

    def copy3(i, h):
        c = handler_chip(core * HF + i, z)
        rows = pl.ds(pl.multiple_of(16 * tile_of(chip, h), 16), 16)
        remote = pltpu.make_async_remote_copy(
            src_ref=g_ref.at[i, :, h], dst_ref=rc3.at[:, rows], send_sem=sem3s.at[i, h], recv_sem=sem3r,
            device_id=at_plane(c, half), device_id_type=MESH,
        )
        local = pltpu.make_async_copy(g_ref.at[i, :, h], rc3.at[:, rows], sem3r)
        return c, remote, local

    for i in range(HF):
        for h in range(2):
            c, remote, local = copy3(i, h)

            @pl.when(c != chip)
            def _():
                remote.start()

            @pl.when(c == chip)
            def _():
                local.start()

    number = handler_number(chip, z) - core * HF
    place = half * HF + number

    def copy4(t):
        h = (t // 4) % 2
        c = (t // 8) * 4 + t % 4
        return pltpu.make_async_remote_copy(
            src_ref=mout.at[t], dst_ref=out_ref.at[place], send_sem=sem4s.at[t], recv_sem=sem4r,
            device_id=at_plane(c, h), device_id_type=MESH,
        )

    own4 = pltpu.make_async_copy(mout.at[tile], out_ref.at[place], sem4r)

    @pl.when((number >= 0) & (number < HF))
    def _():
        pltpu.make_async_copy(rc3, rc3, sem3r).wait()
        for p in range(2):
            wide = rc3[p].astype(F32)
            sym = (0.5 * (wide + wide.T)).astype(BF16)
            s1[p * NG : (p + 1) * NG, :] = sym
            s2[(1 - p) * NG : (2 - p) * NG, :] = sym

        def rows(b, carry):
            at = pl.ds(pl.multiple_of(b * 256, 256), 256)
            at_imag = pl.ds(pl.multiple_of(NG + b * 256, 256), 256)
            real, imag = s1[at, :], s1[at_imag, :]
            m_real = jnp.dot(jnp.concatenate([real, -imag], axis=1), s1[...], preferred_element_type=F32)
            m_imag = jnp.dot(jnp.concatenate([real, imag], axis=1), s2[...], preferred_element_type=F32)
            scale = 1.0 / math.sqrt(NG)
            mout[pl.ds(b * 16, 16), 0] = (m_real * scale).astype(BF16).reshape(16, 16, NG)
            mout[pl.ds(b * 16, 16), 1] = (m_imag * scale).astype(BF16).reshape(16, 16, NG)

            def send(u, carry):
                t = b * 16 + u

                @pl.when(t != tile)
                def _():
                    copy4(t).start()

                @pl.when(t == tile)
                def _():
                    own4.start()

                return carry

            return lax.fori_loop(0, 16, send, carry)

        lax.fori_loop(0, 2, rows, 0)

        def sent(t, carry):
            @pl.when(t != tile)
            def _():
                copy4(t).wait_send()

            return carry

        lax.fori_loop(0, 32, sent, 0)

    def sent1(r, carry):
        copy1((me1 + r) % 32).wait_send()
        return carry

    def sent2(r, carry):
        copy2((chip + r) % 16).wait_send()
        return carry

    lax.fori_loop(1, 32, sent1, 0)
    lax.fori_loop(1, 16, sent2, 0)
    for i in range(HF):
        for h in range(2):
            c, remote, local = copy3(i, h)

            @pl.when(c != chip)
            def _():
                remote.wait_send()

    pltpu.make_async_copy(out_ref, out_ref, sem4r).wait()


def per_device(raw_traces, bin_owner, bin_offset, twiddle):
    vmem = pl.BlockSpec(memory_space=pltpu.VMEM)
    strips = pl.pallas_call(
        kernel,
        out_shape=jax.ShapeDtypeStruct((FB, 2, 16, NG), BF16),
        in_specs=[vmem] * 4,
        out_specs=vmem,
        scratch_shapes=[
            pltpu.VMEM((32, ROWS, CH), BF16),
            pltpu.VMEM((32, ROWS, CH), BF16),
            pltpu.VMEM((512, 4 * CH), BF16),
            pltpu.VMEM((CH, 4 * CH), BF16),
            pltpu.VMEM((2, 512, CH), F32),
            pltpu.VMEM((16, 2, 2, ROWS, CH), BF16),
            pltpu.VMEM((16, 2, 2, ROWS, CH), BF16),
            pltpu.VMEM((HF, 2, 2, 16, NG), BF16),
            pltpu.VMEM((2, NG, NG), BF16),
            pltpu.VMEM((2 * NG, NG), BF16),
            pltpu.VMEM((2 * NG, NG), BF16),
            pltpu.VMEM((NTILE, 2, 16, NG), BF16),
            pltpu.SemaphoreType.DMA((32,)),
            pltpu.SemaphoreType.DMA((32,)),
            pltpu.SemaphoreType.DMA((16,)),
            pltpu.SemaphoreType.DMA((16,)),
            pltpu.SemaphoreType.DMA((HF, 2)),
            pltpu.SemaphoreType.DMA,
            pltpu.SemaphoreType.DMA((32,)),
            pltpu.SemaphoreType.DMA,
        ],
        compiler_params=pltpu.CompilerParams(
            collective_id=0, has_side_effects=True, vmem_limit_bytes=40 * 1024 * 1024
        ),
    )(
        raw_traces.reshape(CH, NT),
        twiddle,
        bin_owner.reshape(32, 128),
        bin_offset.reshape(32, 128),
    )
    return strips.astype(F32)


def solution(mesh):
    table = twiddle_rows()
    step = jax.shard_map(
        per_device,
        mesh=mesh,
        in_specs=(P("tile", "band", None), P("tile", None, None), P("tile", None), P(None, None)),
        out_specs=P("band", None, "tile", None),
        check_vma=False,
    )
    return lambda raw_traces, bin_owner, bin_offset: step(raw_traces, bin_owner, bin_offset, jnp.asarray(table))
```

time: 587 us -> 92.6 us (0.16)
  the two profiles are of different devices: /device:TPU:1 before, /device:TPU:14 now
where the time goes in v1:
time: 92.6 us; the launch traced here: 92.4 us
  Pallas kernels  87.2 us (94%)
  local copies, waits for them, and re-layouts  4.25 us (5%)
    pallas_call x1, Pallas kernels, per_device(): pl.pallas_call(kernel, out_shape=jax.ShapeDtypeStruct((FB, 2, 16, NG), BF...  87.2 us
    unnamed x8, local copies, waits for them, and re-layouts  4.25 us

profile of v1, /device:TPU:14, one launch (start us, length us, event | category | flops | bytes accessed | tf_op | source)
XLA Modules:
  0.0 92.4 jit_solution(7961968213252970886)
XLA Ops:
  0.0 0.0 copy-start
  0.0 1.6 %copy-done = bf16[512,2048]{1,0:T(8,128)(2,1)S(1)} copy-done((bf16[512,2048]{1,0:T(8,128)(2,1)S(1)}, bf16[512,2048]{1,0:T(8,128)(2,1)}, u32[]{:S(2)}) %copy-start) | copy-done | bytes 2097176
  1.6 0.0 copy-start.1
  1.6 1.2 %copy-done.1 = bf16[1,256,2048]{2,1,0:T(8,128)(2,1)S(1)} copy-done((bf16[1,256,2048]{2,1,0:T(8,128)(2,1)S(1)}, bf16[1,256,2048]{2,1,0:T(8,128)(2,1)}, u32[]{:S(2)}) %copy-start.1) | copy-done | bytes 1048600
  2.8 0.0 copy-start.2
  2.8 0.7 copy-done.2
  3.5 0.0 copy-start.3
  3.5 0.7 copy-done.3
  4.3 87.2 %shard_map.46 = bf16[10,2,16,512]{3,2,1,0:T(8,128)(2,1)S(1)} custom-call(bf16[256,2048]{1,0:T(8,128)(2,1)S(1)} %bitcast.3, bf16[512,2048]{1,0:T(8,128)(2,1)S(1)} %copy-done, s32[32,128]{1,0:T(8,128)S(1)} %bitcast.4, s32[32,128]{1,0:T(8,128)S(1)} %bitcast.5), custom_call_target="tpu_custom_call" | custom-call | tf_op jit(solution)/shard_map/pallas_call | solution.py:313
  91.4 0.9 convert_element_type.3
Async XLA Ops:
  0.0 1.6 %copy-start = (bf16[512,2048]{1,0:T(8,128)(2,1)S(1)}, bf16[512,2048]{1,0:T(8,128)(2,1)}, u32[]{:S(2)}) copy-start(bf16[512,2048]{1,0:T(8,128)(2,1)} %constant.2.clone.tw_ref) | copy-start | bytes 6291460
  1.6 1.2 %copy-start.1 = (bf16[1,256,2048]{2,1,0:T(8,128)(2,1)S(1)}, bf16[1,256,2048]{2,1,0:T(8,128)(2,1)}, u32[]{:S(2)}) copy-start(bf16[1,256,2048]{2,1,0:T(8,128)(2,1)} %param.4) | copy-start | bytes 3145732
  2.8 0.7 copy-start.2
  3.5 0.7 copy-start.3

commit v2 on v1

--- a/solution.py
+++ b/solution.py
@@ -31,6 +31,7 @@
                 angle = 2.0 * math.pi * ((time * k) % NT) / NT
                 table[half, band, 2 * i] = np.cos(angle) / math.sqrt(NT)
                 table[half, band, 2 * i + 1] = -np.sin(angle) / math.sqrt(NT)
+    table = np.roll(table.reshape(2 * NB, ROWS, NT), 8, axis=0)
     return table.reshape(2 * NB * ROWS, NT).astype(np.float32).astype(jnp.bfloat16)
 
 
@@ -69,14 +70,33 @@
         r_ref[:, cols] = jnp.where(low == lo_all, BF16(1), BF16(0))
 
 
+def onehot_cells(chunks, l_ref, r_ref):
+    low = lax.broadcasted_iota(jnp.int32, (CH, CH), 0).astype(F32).astype(BF16)
+    keys = lax.broadcasted_iota(jnp.int32, (32, CH), 0).astype(F32).astype(BF16)
+    zero = jnp.zeros((32, CH), BF16)
+    for n, chunk in enumerate(chunks):
+        wide = chunk.astype(F32)
+
+        def spread(row, rows):
+            tile = jnp.broadcast_to(wide[row : row + 1], (ROWS, CH)).astype(BF16)
+            return jnp.concatenate([tile] * (rows // ROWS), axis=0)
+
+        cols = slice(n * CH, (n + 1) * CH)
+        mask = spread(13, 32) == keys
+        for v in range(11):
+            l_ref[v * 32 : (v + 1) * 32, cols] = jnp.where(mask, spread(v, 32), zero)
+        r_ref[:, cols] = jnp.where(low == spread(14, CH), BF16(1), BF16(0))
+
+
 def nt_dot(left, right):
     return lax.dot_general(left, right, (((1,), (1,)), ((), ())), preferred_element_type=F32)
 
 
 def kernel(
-    raw_ref, tw_ref, own_ref, off_ref, out_ref,
+    raw_hbm, tw_hbm, own_hbm, off_hbm, out_ref,
+    raw_ref, tw_ref, own_ref, off_ref,
     send1, rc1, l_ref, r_ref, acc_ref, send2, rc2, g_ref, rc3, s1, s2, mout,
-    sem1s, sem1r, sem2s, sem2r, sem3s, sem3r, sem4s, sem4r,
+    sem_in, sem1s, sem1r, sem2s, sem2r, sem3s, sem3r, sem4s, sem4r,
 ):
     band = lax.axis_index("band")
     tile = lax.axis_index("tile")
@@ -88,29 +108,47 @@
     core = band % 2
     z = half * 8 + zlo
     me1 = half * NB + band
+    part = ((z + 12) % 16) // 8
+    home = ((z + 12) % 8) * 2 + core
 
     def at_column(d):
         return {"band": d % NB, "tile": x * 8 + (d // NB) * 4 + y}
 
-    def at_plane(c, h):
-        return {"band": band, "tile": tile_of(c, h)}
+    def at_plane(c):
+        return {"band": band, "tile": tile_of(c, half)}
+
+    def at_level(c, level):
+        return {"band": (level % 8) * 2 + core, "tile": tile_of(c, level // 8)}
+
+    def column(r):
+        return ((half + r // NB) % 2) * NB + (band + r) % NB
 
     barrier = pltpu.get_barrier_semaphore()
 
     def greet_column(r, carry):
-        d = (me1 + r) % 32
-        pl.semaphore_signal(barrier, inc=1, device_id=at_column(d), device_id_type=MESH)
+        pl.semaphore_signal(barrier, inc=1, device_id=at_column(column(r)), device_id_type=MESH)
         return carry
 
     def greet_plane(r, carry):
         c = (chip + r) % 16
-        pl.semaphore_signal(barrier, inc=1, device_id=at_plane(c, half), device_id_type=MESH)
-        pl.semaphore_signal(barrier, inc=1, device_id=at_plane(c, 1 - half), device_id_type=MESH)
-        return carry
-
+        pl.semaphore_signal(barrier, inc=1, device_id=at_plane(c), device_id_type=MESH)
+        pl.semaphore_signal(barrier, inc=1, device_id=at_level(c, (z + 4) % 16), device_id_type=MESH)
+        pl.semaphore_signal(barrier, inc=1, device_id=at_level(c, (z + 12) % 16), device_id_type=MESH)
+        return carry
+
+    loads = [
+        pltpu.make_async_copy(src, dst, sem_in.at[n])
+        for n, (src, dst) in enumerate(
+            ((own_hbm, own_ref), (off_hbm, off_ref), (raw_hbm, raw_ref), (tw_hbm, tw_ref))
+        )
+    ]
+    for load in loads:
+        load.start()
     lax.fori_loop(1, 32, greet_column, 0)
     lax.fori_loop(1, 16, greet_plane, 0)
 
+    loads[0].wait()
+    loads[1].wait()
     ids = lax.broadcasted_iota(jnp.int32, (32, 128), 0)
 
     def owner_code(t):
@@ -132,17 +170,19 @@
     earlier = jnp.where(earlier, 1.0, 0.0).astype(BF16)
     ahead = jnp.dot(hits.astype(BF16), earlier, preferred_element_type=F32)
     rank = jnp.sum(hits * (ahead + counts), axis=0, keepdims=True)
-    column = off % NG
-    key2 = (column // CH) * 16 + off // NG
+    place = off % NG
+    key2 = (place // CH) * 16 + off // NG
     row_id = lax.broadcasted_iota(jnp.int32, (ROWS, CH), 0)
     labels = jnp.where(row_id == 10, 1.0, 0.0)
-    for at, value in ((11, own.astype(F32)), (12, rank), (13, key2.astype(F32)), (14, (column % CH).astype(F32))):
+    for at, value in ((11, own.astype(F32)), (12, rank), (13, key2.astype(F32)), (14, (place % CH).astype(F32))):
         labels = labels + jnp.where(row_id == at, jnp.broadcast_to(value, (ROWS, CH)), 0.0)
 
+    loads[2].wait()
+    loads[3].wait()
     spectra = nt_dot(tw_ref[...], raw_ref[...]).reshape(2 * NB, ROWS, CH)
     send1[...] = (spectra + labels[None]).astype(BF16)
 
-    pl.semaphore_wait(barrier, 31 + 30)
+    pl.semaphore_wait(barrier, 31 + 45)
 
     def copy1(d):
         return pltpu.make_async_remote_copy(
@@ -151,74 +191,76 @@
         )
 
     def start1(r, carry):
-        copy1((me1 + r) % 32).start()
+        copy1(column(r)).start()
         return carry
 
     own1 = pltpu.make_async_copy(send1.at[me1], rc1.at[me1], sem1r.at[me1])
     own1.start()
     lax.fori_loop(1, 32, start1, 0)
 
-    for lst in range(2):
+    def copy2(s, c):
+        return pltpu.make_async_remote_copy(
+            src_ref=send2.at[s, c], dst_ref=rc2.at[s, chip], send_sem=sem2s.at[s, c], recv_sem=sem2r.at[s, chip],
+            device_id=at_plane(c), device_id_type=MESH,
+        )
+
+    for s in range(2):
+        first = ((half + s) % 2) * NB
+
         def slot(g, carry):
-            for n in range(4):
-                src = lst * NB + g * 4 + n
+            sources = []
+            for n in range(2):
+                k = (1 - s) * 7 + (2 * s - 1) * (g * 2 + n)
+                k = (zlo + 12 + ((k + 1) // 2) * (1 - 2 * (k % 2))) % 8
+                sources += [first + 2 * k, first + 2 * k + 1]
+            for src in sources:
                 pltpu.make_async_copy(rc1.at[src], rc1.at[src], sem1r.at[src]).wait()
-            onehot_groups([rc1[lst * NB + g * 4 + n] for n in range(4)], 11, 12, l_ref, r_ref)
-            part = nt_dot(l_ref[...], r_ref[...])
-            acc_ref[0] += part
+            onehot_groups([rc1[src] for src in sources], 11, 12, l_ref, r_ref)
+            acc_ref[0] += nt_dot(l_ref[...], r_ref[...])
+            return carry
+
+        def start2(r, carry):
+            copy2(s, (chip + r) % 16).start()
             return carry
 
         acc_ref[0] = jnp.zeros((512, CH), F32)
         lax.fori_loop(0, 4, slot, 0)
-        send2[:, :, lst] = acc_ref[0].reshape(16, 2, ROWS, CH).astype(BF16)
-
-    def copy2(c):
-        return pltpu.make_async_remote_copy(
-            src_ref=send2.at[c], dst_ref=rc2.at[chip], send_sem=sem2s.at[c], recv_sem=sem2r.at[chip],
-            device_id=at_plane(c, half), device_id_type=MESH,
-        )
-
-    def start2(r, carry):
-        copy2((chip + r) % 16).start()
-        return carry
-
-    own2 = pltpu.make_async_copy(send2.at[chip], rc2.at[chip], sem2r.at[chip])
-    own2.start()
-    lax.fori_loop(1, 16, start2, 0)
-
-    def bin_group(g, carry):
-        for n in range(2):
-            src = g * 2 + n
-            pltpu.make_async_copy(rc2.at[src], rc2.at[src], sem2r.at[src]).wait()
-        for h in range(2):
-            chunks = [rc2[g * 2 + n // 2, h, n % 2] for n in range(4)]
-            onehot_groups(chunks, 13, 14, l_ref, r_ref)
-            part = nt_dot(l_ref[...], r_ref[...])
-            acc_ref[h] += part
-        return carry
-
-    acc_ref[...] = jnp.zeros_like(acc_ref)
-    lax.fori_loop(0, 8, bin_group, 0)
-    for h in range(2):
-        for hi in range(2):
-            block = acc_ref[h, hi * 256 : (hi + 1) * 256].reshape(16, ROWS, CH)
-            block = block / jnp.maximum(block[:, 10:11, :], 1.0)
-            block = jnp.swapaxes(block, 0, 1).astype(BF16)
-            for v in range(2 * HF):
-                g_ref[v // 2, v % 2, h, :, hi * CH : (hi + 1) * CH] = block[v]
+        send2[s] = acc_ref[0].reshape(16, 2, ROWS, CH).astype(BF16)
+        own2 = pltpu.make_async_copy(send2.at[s, chip], rc2.at[s, chip], sem2r.at[s, chip])
+        own2.start()
+        lax.fori_loop(1, 16, start2, 0)
 
     def copy3(i, h):
         c = handler_chip(core * HF + i, z)
         rows = pl.ds(pl.multiple_of(16 * tile_of(chip, h), 16), 16)
         remote = pltpu.make_async_remote_copy(
             src_ref=g_ref.at[i, :, h], dst_ref=rc3.at[:, rows], send_sem=sem3s.at[i, h], recv_sem=sem3r,
-            device_id=at_plane(c, half), device_id_type=MESH,
+            device_id=at_plane(c), device_id_type=MESH,
         )
         local = pltpu.make_async_copy(g_ref.at[i, :, h], rc3.at[:, rows], sem3r)
         return c, remote, local
 
-    for i in range(HF):
-        for h in range(2):
+    acc_ref[...] = jnp.zeros_like(acc_ref)
+    for s in range(2):
+        def bin_group(g, carry):
+            sources = [(chip + g * 4 + n) % 16 for n in range(4)]
+            for src in sources:
+                pltpu.make_async_copy(rc2.at[s, src], rc2.at[s, src], sem2r.at[s, src]).wait()
+            for h in range(2):
+                onehot_cells([rc2[s, src, h] for src in sources], l_ref, r_ref)
+                acc_ref[h, :352] += nt_dot(l_ref[:352], r_ref[...])
+            return carry
+
+        lax.fori_loop(0, 4, bin_group, 0)
+
+    for h in range(2):
+        for hi in range(2):
+            many = acc_ref[h, 320 + hi * 16 : 336 + hi * 16, :]
+            share = 1.0 / jnp.maximum(many, 1.0)
+            for v in range(2 * HF):
+                mean = acc_ref[h, v * 32 + hi * 16 : v * 32 + hi * 16 + 16, :] * share
+                g_ref[v // 2, v % 2, h, :, hi * CH : (hi + 1) * CH] = mean.astype(BF16)
+        for i in range(HF):
             c, remote, local = copy3(i, h)
 
             @pl.when(c != chip)
@@ -230,17 +272,13 @@
                 local.start()
 
     number = handler_number(chip, z) - core * HF
-    place = half * HF + number
+    place4 = part * HF + number
 
     def copy4(t):
-        h = (t // 4) % 2
-        c = (t // 8) * 4 + t % 4
         return pltpu.make_async_remote_copy(
-            src_ref=mout.at[t], dst_ref=out_ref.at[place], send_sem=sem4s.at[t], recv_sem=sem4r,
-            device_id=at_plane(c, h), device_id_type=MESH,
-        )
-
-    own4 = pltpu.make_async_copy(mout.at[tile], out_ref.at[place], sem4r)
+            src_ref=mout.at[t], dst_ref=out_ref.at[place4], send_sem=sem4s.at[t], recv_sem=sem4r,
+            device_id={"band": home, "tile": t}, device_id_type=MESH,
+        )
 
     @pl.when((number >= 0) & (number < HF))
     def _():
@@ -262,16 +300,7 @@
             mout[pl.ds(b * 16, 16), 1] = (m_imag * scale).astype(BF16).reshape(16, 16, NG)
 
             def send(u, carry):
-                t = b * 16 + u
-
-                @pl.when(t != tile)
-                def _():
-                    copy4(t).start()
-
-                @pl.when(t == tile)
-                def _():
-                    own4.start()
-
+                copy4(tile_of(b * 8 + (chip + u // 2) % 8, u % 2)).start()
                 return carry
 
             return lax.fori_loop(0, 16, send, carry)
@@ -279,20 +308,18 @@
         lax.fori_loop(0, 2, rows, 0)
 
         def sent(t, carry):
-            @pl.when(t != tile)
-            def _():
-                copy4(t).wait_send()
-
+            copy4(t).wait_send()
             return carry
 
         lax.fori_loop(0, 32, sent, 0)
 
     def sent1(r, carry):
-        copy1((me1 + r) % 32).wait_send()
+        copy1(column(r)).wait_send()
         return carry
 
     def sent2(r, carry):
-        copy2((chip + r) % 16).wait_send()
+        copy2(0, (chip + r) % 16).wait_send()
+        copy2(1, (chip + r) % 16).wait_send()
         return carry
 
     lax.fori_loop(1, 32, sent1, 0)
@@ -310,35 +337,41 @@
 
 def per_device(raw_traces, bin_owner, bin_offset, twiddle):
     vmem = pl.BlockSpec(memory_space=pltpu.VMEM)
+    anywhere = pl.BlockSpec(memory_space=pltpu.HBM)
     strips = pl.pallas_call(
         kernel,
         out_shape=jax.ShapeDtypeStruct((FB, 2, 16, NG), BF16),
-        in_specs=[vmem] * 4,
+        in_specs=[anywhere] * 4,
         out_specs=vmem,
         scratch_shapes=[
+            pltpu.VMEM((CH, NT), BF16),
+            pltpu.VMEM((2 * NB * ROWS, NT), BF16),
+            pltpu.VMEM((32, 128), jnp.int32),
+            pltpu.VMEM((32, 128), jnp.int32),
             pltpu.VMEM((32, ROWS, CH), BF16),
             pltpu.VMEM((32, ROWS, CH), BF16),
             pltpu.VMEM((512, 4 * CH), BF16),
             pltpu.VMEM((CH, 4 * CH), BF16),
             pltpu.VMEM((2, 512, CH), F32),
-            pltpu.VMEM((16, 2, 2, ROWS, CH), BF16),
-            pltpu.VMEM((16, 2, 2, ROWS, CH), BF16),
+            pltpu.VMEM((2, 16, 2, ROWS, CH), BF16),
+            pltpu.VMEM((2, 16, 2, ROWS, CH), BF16),
             pltpu.VMEM((HF, 2, 2, 16, NG), BF16),
             pltpu.VMEM((2, NG, NG), BF16),
             pltpu.VMEM((2 * NG, NG), BF16),
             pltpu.VMEM((2 * NG, NG), BF16),
             pltpu.VMEM((NTILE, 2, 16, NG), BF16),
+            pltpu.SemaphoreType.DMA((4,)),
             pltpu.SemaphoreType.DMA((32,)),
             pltpu.SemaphoreType.DMA((32,)),
-            pltpu.SemaphoreType.DMA((16,)),
-            pltpu.SemaphoreType.DMA((16,)),
+            pltpu.SemaphoreType.DMA((2, 16)),
+            pltpu.SemaphoreType.DMA((2, 16)),
             pltpu.SemaphoreType.DMA((HF, 2)),
             pltpu.SemaphoreType.DMA,
             pltpu.SemaphoreType.DMA((32,)),
             pltpu.SemaphoreType.DMA,
         ],
         compiler_params=pltpu.CompilerParams(
-            collective_id=0, has_side_effects=True, vmem_limit_bytes=40 * 1024 * 1024
+            collective_id=0, has_side_effects=True, vmem_limit_bytes=60 * 1024 * 1024
         ),
     )(
         raw_traces.reshape(CH, NT),

time: 92.6 us -> 78 us (0.84)
  the two profiles are of different devices: /device:TPU:14 before, /device:TPU:28 now
where the time goes in v2:
time: 78 us; the launch traced here: 77.9 us
  Pallas kernels  76 us (97%)
  other arithmetic  1.88 us (2%)
    pallas_call x1, Pallas kernels, per_device(): pl.pallas_call(kernel, out_shape=jax.ShapeDtypeStruct((FB, 2, 16, NG), BF...  76 us
    convert_element_type x1, other arithmetic, per_device(): return strips.astype(F32)  1.88 us

profile of v2, /device:TPU:28, one launch (start us, length us, event | category | flops | bytes accessed | tf_op | source)
XLA Modules:
  0.0 77.9 jit_solution(7486557280486576612)
XLA Ops:
  0.0 76.0 %shard_map.46 = bf16[10,2,16,512]{3,2,1,0:T(8,128)(2,1)} custom-call(bf16[256,2048]{1,0:T(8,128)(2,1)} %bitcast.3, bf16[512,2048]{1,0:T(8,128)(2,1)} %constant.2.clone.tw_hbm, s32[32,128]{1,0:T(8,128)} %bitcast.4, s32[32,128]{1,0:T(8,128)} %bitcast.5), custom_call_target="tpu_custom_call" | custom-call | tf_op jit(solution)/shard_map/pallas_call | solution.py:341
  76.0 1.9 %convert_element_type.3 = f32[10,2,16,512]{3,2,1,0:T(8,128)} convert(bf16[10,2,16,512]{3,2,1,0:T(8,128)(2,1)} %shard_map.46) | non-fusion elementwise | flops 163840 | bytes 983040 | tf_op jit(solution)/shard_map/convert_element_type | solution.py:382

commit v3 on v2

--- a/solution.py
+++ b/solution.py
@@ -40,7 +40,7 @@
 
 
 def shift_of(z):
-    return (z * 5) % 16
+    return (z * 4) % 16
 
 
 def handler_chip(n, z):
@@ -191,12 +191,17 @@
         )
 
     def start1(r, carry):
-        copy1(column(r)).start()
+        d = (((half + (r // 8) % 2) % 2) * 8 + (zlo + r % 8) % 8) * 2 + r // 16
+
+        @pl.when(d != me1)
+        def _():
+            copy1(d).start()
+
         return carry
 
     own1 = pltpu.make_async_copy(send1.at[me1], rc1.at[me1], sem1r.at[me1])
     own1.start()
-    lax.fori_loop(1, 32, start1, 0)
+    lax.fori_loop(0, 32, start1, 0)
 
     def copy2(s, c):
         return pltpu.make_async_remote_copy(
@@ -220,7 +225,10 @@
             return carry
 
         def start2(r, carry):
-            copy2(s, (chip + r) % 16).start()
+            q = r % 4
+            dx = (2 + 4 - r // 4 + (r // 8) * (7 - 2 * (r // 4))) % 4
+            dy = (2 + 4 - q + (q // 2) * (7 - 2 * q)) % 4
+            copy2(s, ((x + dx) % 4) * 4 + (y + dy) % 4).start()
             return carry
 
         acc_ref[0] = jnp.zeros((512, CH), F32)
@@ -228,17 +236,21 @@
         send2[s] = acc_ref[0].reshape(16, 2, ROWS, CH).astype(BF16)
         own2 = pltpu.make_async_copy(send2.at[s, chip], rc2.at[s, chip], sem2r.at[s, chip])
         own2.start()
-        lax.fori_loop(1, 16, start2, 0)
+        lax.fori_loop(0, 15, start2, 0)
 
     def copy3(i, h):
-        c = handler_chip(core * HF + i, z)
         rows = pl.ds(pl.multiple_of(16 * tile_of(chip, h), 16), 16)
+        if i < 4:
+            freq, level, c = i, z, handler_chip(core * 4 + i, z)
+        else:
+            level = (z + 4 + 8 * (i - 4)) % 16
+            freq, c = 4, handler_chip(8 + core * 2 + i - 4, level)
         remote = pltpu.make_async_remote_copy(
-            src_ref=g_ref.at[i, :, h], dst_ref=rc3.at[:, rows], send_sem=sem3s.at[i, h], recv_sem=sem3r,
-            device_id=at_plane(c), device_id_type=MESH,
-        )
-        local = pltpu.make_async_copy(g_ref.at[i, :, h], rc3.at[:, rows], sem3r)
-        return c, remote, local
+            src_ref=g_ref.at[freq, :, h], dst_ref=rc3.at[:, rows], send_sem=sem3s.at[i, h], recv_sem=sem3r,
+            device_id=at_level(c, level), device_id_type=MESH,
+        )
+        local = pltpu.make_async_copy(g_ref.at[freq, :, h], rc3.at[:, rows], sem3r)
+        return (c == chip) & (level == z), remote, local
 
     acc_ref[...] = jnp.zeros_like(acc_ref)
     for s in range(2):
@@ -260,27 +272,49 @@
             for v in range(2 * HF):
                 mean = acc_ref[h, v * 32 + hi * 16 : v * 32 + hi * 16 + 16, :] * share
                 g_ref[v // 2, v % 2, h, :, hi * CH : (hi + 1) * CH] = mean.astype(BF16)
-        for i in range(HF):
-            c, remote, local = copy3(i, h)
-
-            @pl.when(c != chip)
+        for i in (4, 5, 0, 1, 2, 3):
+            here, remote, local = copy3(i, h)
+            if i >= 4:
+                remote.start()
+                continue
+
+            @pl.when(jnp.logical_not(here))
             def _():
                 remote.start()
 
-            @pl.when(c == chip)
+            @pl.when(here)
             def _():
                 local.start()
 
-    number = handler_number(chip, z) - core * HF
-    place4 = part * HF + number
+    number = handler_number(chip, z)
+    far = number - core * 4
+    near = number - 8 - core * 2
+    is_far = (far >= 0) & (far < 4)
+    is_near = (near >= 0) & (near < 2)
+    far_place = part * HF + far
+    near_place = ((half + 1 + near) % 2) * HF + 4
+
+    def product(real, imag):
+        m_real = jnp.dot(jnp.concatenate([real, -imag], axis=1), s1[...], preferred_element_type=F32)
+        m_imag = jnp.dot(jnp.concatenate([real, imag], axis=1), s2[...], preferred_element_type=F32)
+        scale = 1.0 / math.sqrt(NG)
+        return [(m * scale).astype(BF16).reshape(16, 16, NG) for m in (m_real, m_imag)]
 
     def copy4(t):
         return pltpu.make_async_remote_copy(
-            src_ref=mout.at[t], dst_ref=out_ref.at[place4], send_sem=sem4s.at[t], recv_sem=sem4r,
+            src_ref=mout.at[t], dst_ref=out_ref.at[far_place], send_sem=sem4s.at[t], recv_sem=sem4r,
             device_id={"band": home, "tile": t}, device_id_type=MESH,
         )
 
-    @pl.when((number >= 0) & (number < HF))
+    def copy5(c):
+        return pltpu.make_async_remote_copy(
+            src_ref=mout.at[c], dst_ref=out_ref.at[near_place], send_sem=sem4s.at[c], recv_sem=sem4r,
+            device_id=at_plane(c), device_id_type=MESH,
+        )
+
+    own5 = pltpu.make_async_copy(mout.at[chip], out_ref.at[near_place], sem4r)
+
+    @pl.when(is_far | is_near)
     def _():
         pltpu.make_async_copy(rc3, rc3, sem3r).wait()
         for p in range(2):
@@ -289,18 +323,20 @@
             s1[p * NG : (p + 1) * NG, :] = sym
             s2[(1 - p) * NG : (2 - p) * NG, :] = sym
 
-        def rows(b, carry):
+    @pl.when(is_far)
+    def _():
+        def rows(turn, carry):
+            b = (x // 2 + 1 + turn) % 2
             at = pl.ds(pl.multiple_of(b * 256, 256), 256)
             at_imag = pl.ds(pl.multiple_of(NG + b * 256, 256), 256)
-            real, imag = s1[at, :], s1[at_imag, :]
-            m_real = jnp.dot(jnp.concatenate([real, -imag], axis=1), s1[...], preferred_element_type=F32)
-            m_imag = jnp.dot(jnp.concatenate([real, imag], axis=1), s2[...], preferred_element_type=F32)
-            scale = 1.0 / math.sqrt(NG)
-            mout[pl.ds(b * 16, 16), 0] = (m_real * scale).astype(BF16).reshape(16, 16, NG)
-            mout[pl.ds(b * 16, 16), 1] = (m_imag * scale).astype(BF16).reshape(16, 16, NG)
+            for p, m in enumerate(product(s1[at, :], s1[at_imag, :])):
+                mout[pl.ds(b * 16, 16), p] = m
 
             def send(u, carry):
-                copy4(tile_of(b * 8 + (chip + u // 2) % 8, u % 2)).start()
+                q = u // 4
+                up = (y + 2 + 4 - q + (q // 2) * (7 - 2 * q)) % 4
+                along = 2 * b + (x + 1 + (u // 2) % 2) % 2
+                copy4(tile_of(along * 4 + up, u % 2)).start()
                 return carry
 
             return lax.fori_loop(0, 16, send, carry)
@@ -312,6 +348,25 @@
             return carry
 
         lax.fori_loop(0, 32, sent, 0)
+
+    @pl.when(is_near)
+    def _():
+        real = [s1[pl.ds(pl.multiple_of(128 * n + 64 * half, 64), 64), :] for n in range(4)]
+        imag = [s1[pl.ds(pl.multiple_of(NG + 128 * n + 64 * half, 64), 64), :] for n in range(4)]
+        for p, m in enumerate(product(jnp.concatenate(real, axis=0), jnp.concatenate(imag, axis=0))):
+            mout[:16, p] = m
+        own5.start()
+
+        def send(r, carry):
+            copy5((chip + r) % 16).start()
+            return carry
+
+        def sent(r, carry):
+            copy5((chip + r) % 16).wait_send()
+            return carry
+
+        lax.fori_loop(1, 16, send, 0)
+        lax.fori_loop(1, 16, sent, 0)
 
     def sent1(r, carry):
         copy1(column(r)).wait_send()
@@ -324,11 +379,14 @@
 
     lax.fori_loop(1, 32, sent1, 0)
     lax.fori_loop(1, 16, sent2, 0)
-    for i in range(HF):
+    for i in range(6):
         for h in range(2):
-            c, remote, local = copy3(i, h)
-
-            @pl.when(c != chip)
+            here, remote, local = copy3(i, h)
+            if i >= 4:
+                remote.wait_send()
+                continue
+
+            @pl.when(jnp.logical_not(here))
             def _():
                 remote.wait_send()
 
@@ -365,7 +423,7 @@
             pltpu.SemaphoreType.DMA((32,)),
             pltpu.SemaphoreType.DMA((2, 16)),
             pltpu.SemaphoreType.DMA((2, 16)),
-            pltpu.SemaphoreType.DMA((HF, 2)),
+            pltpu.SemaphoreType.DMA((6, 2)),
             pltpu.SemaphoreType.DMA,
             pltpu.SemaphoreType.DMA((32,)),
             pltpu.SemaphoreType.DMA,

time: 78 us -> 70.8 us (0.908)
  the two profiles are of different devices: /device:TPU:28 before, /device:TPU:1 now
where the time goes in v3:
time: 70.8 us; the launch traced here: 70.6 us
  Pallas kernels  68.7 us (97%)
  other arithmetic  1.88 us (3%)
    pallas_call x1, Pallas kernels, per_device(): pl.pallas_call(kernel, out_shape=jax.ShapeDtypeStruct((FB, 2, 16, NG), BF...  68.7 us
    convert_element_type x1, other arithmetic, per_device(): return strips.astype(F32)  1.88 us

profile of v3, /device:TPU:1, one launch (start us, length us, event | category | flops | bytes accessed | tf_op | source)
XLA Modules:
  0.0 70.6 jit_solution(8759717857821425442)
XLA Ops:
  0.0 68.7 %shard_map.46 = bf16[10,2,16,512]{3,2,1,0:T(8,128)(2,1)} custom-call(bf16[256,2048]{1,0:T(8,128)(2,1)} %bitcast.3, bf16[512,2048]{1,0:T(8,128)(2,1)} %constant.2.clone.tw_hbm, s32[32,128]{1,0:T(8,128)} %bitcast.4, s32[32,128]{1,0:T(8,128)} %bitcast.5), custom_call_target="tpu_custom_call" | custom-call | tf_op jit(solution)/shard_map/pallas_call | solution.py:399
  68.7 1.9 %convert_element_type.3 = f32[10,2,16,512]{3,2,1,0:T(8,128)} convert(bf16[10,2,16,512]{3,2,1,0:T(8,128)(2,1)} %shard_map.46) | non-fusion elementwise | flops 163840 | bytes 983040 | tf_op jit(solution)/shard_map/convert_element_type | solution.py:440

commit v4 on v3

--- a/solution.py
+++ b/solution.py
@@ -132,8 +132,6 @@
     def greet_plane(r, carry):
         c = (chip + r) % 16
         pl.semaphore_signal(barrier, inc=1, device_id=at_plane(c), device_id_type=MESH)
-        pl.semaphore_signal(barrier, inc=1, device_id=at_level(c, (z + 4) % 16), device_id_type=MESH)
-        pl.semaphore_signal(barrier, inc=1, device_id=at_level(c, (z + 12) % 16), device_id_type=MESH)
         return carry
 
     loads = [
@@ -182,7 +180,7 @@
     spectra = nt_dot(tw_ref[...], raw_ref[...]).reshape(2 * NB, ROWS, CH)
     send1[...] = (spectra + labels[None]).astype(BF16)
 
-    pl.semaphore_wait(barrier, 31 + 45)
+    pl.semaphore_wait(barrier, 31 + 15)
 
     def copy1(d):
         return pltpu.make_async_remote_copy(
@@ -191,7 +189,9 @@
         )
 
     def start1(r, carry):
-        d = (((half + (r // 8) % 2) % 2) * 8 + (zlo + r % 8) % 8) * 2 + r // 16
+        k = r % 8
+        turn = (((k + 1) // 2) * (1 - 2 * (k % 2)) + 8) % 8
+        d = (((half + (r // 8) % 2) % 2) * 8 + (zlo + turn) % 8) * 2 + r // 16
 
         @pl.when(d != me1)
         def _():

time: 70.8 us -> 69.2 us (0.977)
  Pallas kernels: 68.7 us -> 66.4 us
    pallas_call x1, Pallas kernels: 68.7 us -> 66.4 us  [per_device(): pl.pallas_call(kernel, out_shape=jax.ShapeDtypeStruct((FB, 2, 16, NG), BF...]
where the time goes in v4:
time: 69.2 us; the launch traced here: 68.3 us
  Pallas kernels  66.4 us (96%)
  other arithmetic  1.88 us (3%)
    pallas_call x1, Pallas kernels, per_device(): pl.pallas_call(kernel, out_shape=jax.ShapeDtypeStruct((FB, 2, 16, NG), BF...  66.4 us
    convert_element_type x1, other arithmetic, per_device(): return strips.astype(F32)  1.88 us

profile of v4, /device:TPU:1, one launch (start us, length us, event | category | flops | bytes accessed | tf_op | source)
XLA Modules:
  0.0 68.3 jit_solution(13590479290480181906)
XLA Ops:
  0.0 66.4 %shard_map.46 = bf16[10,2,16,512]{3,2,1,0:T(8,128)(2,1)} custom-call(bf16[256,2048]{1,0:T(8,128)(2,1)} %bitcast.3, bf16[512,2048]{1,0:T(8,128)(2,1)} %constant.2.clone.tw_hbm, s32[32,128]{1,0:T(8,128)} %bitcast.4, s32[32,128]{1,0:T(8,128)} %bitcast.5), custom_call_target="tpu_custom_call" | custom-call | tf_op jit(solution)/shard_map/pallas_call | solution.py:399
  66.4 1.9 %convert_element_type.3 = f32[10,2,16,512]{3,2,1,0:T(8,128)} convert(bf16[10,2,16,512]{3,2,1,0:T(8,128)(2,1)} %shard_map.46) | non-fusion elementwise | flops 163840 | bytes 983040 | tf_op jit(solution)/shard_map/convert_element_type | solution.py:440

commit v5 on v4

--- a/solution.py
+++ b/solution.py
@@ -220,8 +220,8 @@
                 sources += [first + 2 * k, first + 2 * k + 1]
             for src in sources:
                 pltpu.make_async_copy(rc1.at[src], rc1.at[src], sem1r.at[src]).wait()
-            onehot_groups([rc1[src] for src in sources], 11, 12, l_ref, r_ref)
-            acc_ref[0] += nt_dot(l_ref[...], r_ref[...])
+            onehot_groups([rc1[src] for src in sources], 11, 12, l_ref.at[0], r_ref.at[0])
+            acc_ref[0] += nt_dot(l_ref[0], r_ref[0])
             return carry
 
         def start2(r, carry):
@@ -259,8 +259,8 @@
             for src in sources:
                 pltpu.make_async_copy(rc2.at[s, src], rc2.at[s, src], sem2r.at[s, src]).wait()
             for h in range(2):
-                onehot_cells([rc2[s, src, h] for src in sources], l_ref, r_ref)
-                acc_ref[h, :352] += nt_dot(l_ref[:352], r_ref[...])
+                onehot_cells([rc2[s, src, h] for src in sources], l_ref.at[h], r_ref.at[h])
+                acc_ref[h, :352] += nt_dot(l_ref[h, :352], r_ref[h])
             return carry
 
         lax.fori_loop(0, 4, bin_group, 0)
@@ -408,8 +408,8 @@
             pltpu.VMEM((32, 128), jnp.int32),
             pltpu.VMEM((32, ROWS, CH), BF16),
             pltpu.VMEM((32, ROWS, CH), BF16),
-            pltpu.VMEM((512, 4 * CH), BF16),
-            pltpu.VMEM((CH, 4 * CH), BF16),
+            pltpu.VMEM((2, 512, 4 * CH), BF16),
+            pltpu.VMEM((2, CH, 4 * CH), BF16),
             pltpu.VMEM((2, 512, CH), F32),
             pltpu.VMEM((2, 16, 2, ROWS, CH), BF16),
             pltpu.VMEM((2, 16, 2, ROWS, CH), BF16),

time: 69.2 us -> 69.1 us (level)
  no operation moved by 1% of the time
where the time goes in v5:
time: 69.1 us; the launch traced here: 68.3 us
  Pallas kernels  66.4 us (96%)
  other arithmetic  1.88 us (3%)
    pallas_call x1, Pallas kernels, per_device(): pl.pallas_call(kernel, out_shape=jax.ShapeDtypeStruct((FB, 2, 16, NG), BF...  66.4 us
    convert_element_type x1, other arithmetic, per_device(): return strips.astype(F32)  1.88 us

profile of v5, /device:TPU:1, one launch (start us, length us, event | category | flops | bytes accessed | tf_op | source)
XLA Modules:
  0.0 68.3 jit_solution(12506817009639129460)
XLA Ops:
  0.0 66.4 %shard_map.46 = bf16[10,2,16,512]{3,2,1,0:T(8,128)(2,1)} custom-call(bf16[256,2048]{1,0:T(8,128)(2,1)} %bitcast.3, bf16[512,2048]{1,0:T(8,128)(2,1)} %constant.2.clone.tw_hbm, s32[32,128]{1,0:T(8,128)} %bitcast.4, s32[32,128]{1,0:T(8,128)} %bitcast.5), custom_call_target="tpu_custom_call" | custom-call | tf_op jit(solution)/shard_map/pallas_call | solution.py:399
  66.4 1.9 %convert_element_type.3 = f32[10,2,16,512]{3,2,1,0:T(8,128)} convert(bf16[10,2,16,512]{3,2,1,0:T(8,128)(2,1)} %shard_map.46) | non-fusion elementwise | flops 163840 | bytes 983040 | tf_op jit(solution)/shard_map/convert_element_type | solution.py:440
